TPU v7x, 32 devices: a whole 2x2x4 slice. The times are simulated.
32 devices in a mesh: groups: 2 (over x), seq: 16 (over z, y, core).
Axes of the slice: x: 2, y: 2, z: 4, core: 2. Of those that a mesh axis runs over, the one named last changes fastest.
Arguments:
- queries: bfloat16 [1024, 2048], P(('groups', 'seq')), parts along dimension 0, may hold values from -2048 to 2048
- new_keys: bfloat16 [1024, 512], P(('groups', 'seq')), parts along dimension 0, may hold values from -16 to 16
- new_values: bfloat16 [1024, 512], P(('groups', 'seq')), parts along dimension 0, may hold values from -6 to 6
- keys: bfloat16 [131072, 512], P(('groups', 'seq')), parts along dimension 0, may hold values from -16 to 16
- values: bfloat16 [131072, 512], P(('groups', 'seq')), parts along dimension 0, may hold values from -6 to 6
- page_list: int32 [256, 3], P(('groups', 'seq')), parts along dimension 0, may hold values from 0 to 15, as said below
- out_weight: bfloat16 [2048, 4096], P(None, 'seq'), may hold values from -0.125 to 0.125
Outputs:
- projected: bfloat16 [1024, 4096], P(('groups', 'seq')), parts along dimension 0
There are 2 independent parts, one for each index of `groups`. A program takes and returns all parts, laid end to end along the dimension named above; an argument that names none is the same for every part. Nothing has to cross between parts.
Inputs may be any that keep to these rules, and one draw needn't show every extreme that they name: `page_list`: the 3 pages of a tile are distinct. Among the 8 tiles of one index of seq (tiles 8 * i to 8 * (i + 1) - 1) no page is listed more than 3 times, and some page is listed exactly 3 times by the tiles of every index.
All inputs are finite; a program needn't handle non-finite values.
Results may differ from a plain program's by a relative error of at most 0.0058.
Values may be sent and summed in bfloat16 or wider, within the bound.
A program may use at most 192 MiB of HBM per device.

v0:
```python
import math

import jax
import jax.numpy as jnp
from jax import lax
from jax.sharding import PartitionSpec as P

HQ = 16
KVH = 4
HD = 128


def shards(queries, new_keys, new_values, keys, values, page_list, out_weight):
    members = lax.axis_size("seq")
    tile_count, list_width = page_list.shape
    row_total, features = queries.shape
    tile_rows = row_total // tile_count
    per_group = HQ // KVH
    capacity = max(1, 2 * tile_count * list_width // members)
    slot_count = members * capacity
    order_ids = jnp.arange(tile_count)
    before = order_ids[None, :] < order_ids[:, None]
    matches = page_list[:, :, None, None] == page_list[None, None, :, :]
    ranking = jnp.sum(matches & before[:, None, :, None], axis=(2, 3))
    slot_index = page_list * capacity + ranking
    placing = jnp.any(
        slot_index[:, :, None] == jnp.arange(slot_count, dtype=jnp.int32)[None, None, :], axis=1
    )
    placing = placing.astype(jnp.bfloat16)
    outgoing = lax.dot_general(
        placing,
        queries.reshape(tile_count, tile_rows * features),
        (((0,), (0,)), ((), ())),
        preferred_element_type=jnp.float32,
    )
    outgoing = outgoing.astype(jnp.bfloat16).reshape(members, capacity, tile_rows, features)
    incoming = lax.all_to_all(outgoing, "seq", split_axis=0, concat_axis=0, tiled=True)
    layout = incoming.shape
    row_count = layout[0] * layout[1] * layout[2]
    flattened = incoming.reshape(row_count, features)
    pieces = []
    maxima = []
    totals = []
    for head_group in range(KVH):
        column_start = head_group * per_group * HD
        asked = flattened[:, column_start : column_start + per_group * HD].reshape(
            row_count * per_group, HD
        )
        cached_keys = keys[:, head_group * HD : (head_group + 1) * HD]
        cached_values = values[:, head_group * HD : (head_group + 1) * HD]
        scores = lax.dot_general(
            asked, cached_keys, (((1,), (1,)), ((), ())), preferred_element_type=jnp.float32
        ) / math.sqrt(HD)
        highest = jnp.max(scores, axis=1, keepdims=True)
        weights = jnp.exp(scores - highest)
        summed = jnp.sum(weights, axis=1, keepdims=True)
        mixed = (
            jnp.dot(weights.astype(jnp.bfloat16), cached_values, preferred_element_type=jnp.float32)
            / summed
        )
        pieces.append(mixed.reshape(row_count, per_group * HD))
        maxima.append(highest.reshape(row_count, per_group))
        totals.append(summed.reshape(row_count, per_group))
    partial_out = jnp.concatenate(pieces, axis=1).astype(jnp.bfloat16).reshape(layout)
    stat_shape = layout[:3] + (HQ,)
    maxima_all = jnp.concatenate(maxima, axis=1).reshape(stat_shape)
    totals_all = jnp.concatenate(totals, axis=1).reshape(stat_shape)
    returned = lax.all_to_all(partial_out, "seq", split_axis=0, concat_axis=0, tiled=True)
    returned_max = lax.all_to_all(maxima_all, "seq", split_axis=0, concat_axis=0, tiled=True)
    returned_total = lax.all_to_all(totals_all, "seq", split_axis=0, concat_axis=0, tiled=True)
    returned, returned_max, returned_total = (returned, returned_max, returned_total)
    asked_local = queries.reshape(tile_count, tile_rows, KVH, per_group, HD)
    fresh_keys = new_keys.reshape(tile_count, tile_rows, KVH, HD)
    fresh_values = new_values.reshape(tile_count, tile_rows, KVH, HD)
    own_scores = jnp.einsum(
        "tqgjd,tkgd->tqgjk", asked_local, fresh_keys, preferred_element_type=jnp.float32
    ) / math.sqrt(HD)
    causal = jnp.arange(tile_rows)[:, None] >= jnp.arange(tile_rows)[None, :]
    own_scores = jnp.where(causal[None, :, None, None, :], own_scores, -jnp.inf)
    own_max = jnp.max(own_scores, axis=-1)
    own_weights = jnp.exp(own_scores - own_max[..., None])
    own_total = jnp.sum(own_weights, axis=-1)
    own_out = (
        jnp.einsum(
            "tqgjk,tkgd->tqgjd",
            own_weights.astype(jnp.bfloat16),
            fresh_values,
            preferred_element_type=jnp.float32,
        )
        / own_total[..., None]
    )
    own_out = own_out.reshape(tile_count, tile_rows, HQ, HD)
    own_max = own_max.reshape(tile_count, tile_rows, HQ)
    own_total = own_total.reshape(tile_count, tile_rows, HQ)
    got_out = returned.reshape(slot_count, tile_rows, HQ, HD)
    got_max = returned_max.reshape(slot_count, tile_rows, HQ)
    got_total = returned_total.reshape(slot_count, tile_rows, HQ)
    chosen_out = got_out[slot_index].astype(jnp.float32)
    chosen_max = got_max[slot_index]
    chosen_total = got_total[slot_index]
    overall = jnp.maximum(own_max, jnp.max(chosen_max, axis=1))
    own_factor = own_total * jnp.exp(own_max - overall)
    page_factor = chosen_total * jnp.exp(chosen_max - overall[:, None])
    denom = own_factor + jnp.sum(page_factor, axis=1)
    numer = own_factor[..., None] * own_out + jnp.sum(page_factor[..., None] * chosen_out, axis=1)
    attended = (numer / denom[..., None]).reshape(row_total, features).astype(jnp.bfloat16)
    return jnp.dot(
        attended,
        lax.all_gather(out_weight, "seq", axis=1, tiled=True),
        preferred_element_type=jnp.float32,
    ).astype(jnp.bfloat16)


def solution(mesh):
    return jax.shard_map(
        shards,
        mesh=mesh,
        in_specs=(
            P(("groups", "seq"), None),
            P(("groups", "seq"), None),
            P(("groups", "seq"), None),
            P(("groups", "seq"), None),
            P(("groups", "seq"), None),
            P(("groups", "seq"), None),
            P(None, "seq"),
        ),
        out_specs=P(("groups", "seq"), None),
        check_vma=False,
    )
```

profile of v0, /device:TPU:0, one launch (start us, length us, event | category | flops | bytes accessed | tf_op | source)
XLA Modules:
  0.0 197.4 jit_solution(5072526256052859871)
XLA Ops:
  7.3 1.0 reshape.173
  8.3 1.0 convert_reduce_fusion
  11.0 44.6 %all_to_all.20 = bf16[16,3,4,2048]{3,2,1,0:T(4,128)(2,1)S(1)} all-to-all(bf16[16,3,4,2048]{3,2,1,0:T(4,128)(2,1)S(1)} %reshape.174), channel_id=1, replica_groups=mesh['groups'=2,'seq'=16] {'seq'}, dimensions={0} | all-to-all | bytes 1572864 | tf_op jit(solution)/shard_map/all_to_all | solution.py:37
  56.4 7.6 %multiply_reduce_fusion.2 = (f32[768]{0:T(1024)S(1)}, f32[768,4096]{1,0:T(8,128)}) fusion(bf16[768,128]{1,0:T(8,128)(2,1)S(1)} %reshape.177, bf16[4096,512]{1,0:T(8,128)(2,1)} %param.10), kind=kOutput, calls=%fused_computation.9 | convolution fusion | flops 811597056 | bytes 13831168 | tf_op jit(solution)/shard_map/dot_general | solution.py:51
  64.2 6.8 %fusion.3 = f32[768]{0:T(1024)S(1)} fusion(f32[768,4096]{1,0:T(8,128)} %get-tuple-element.20, f32[768]{0:T(1024)S(1)} %get-tuple-element.19), kind=kLoop, calls=%fused_computation.14 | loop fusion | flops 9436416 | bytes 12589056 | tf_op jit(solution)/shard_map/reduce_sum | solution.py:56
  71.1 7.5 %multiply_reduce_fusion.1 = (f32[768]{0:T(1024)S(1)}, f32[768,4096]{1,0:T(8,128)}) fusion(bf16[768,128]{1,0:T(8,128)(2,1)S(1)} %reshape.178, bf16[4096,512]{1,0:T(8,128)(2,1)} %param.10), kind=kOutput, calls=%fused_computation.8 | convolution fusion | flops 811597056 | bytes 13831168 | tf_op jit(solution)/shard_map/dot_general | solution.py:51
  78.7 8.2 %fusion.5 = f32[768]{0:T(1024)S(1)} fusion(f32[768,4096]{1,0:T(8,128)} %get-tuple-element.18, f32[768]{0:T(1024)S(1)} %get-tuple-element.17), kind=kLoop, calls=%fused_computation.16 | loop fusion | flops 9436416 | bytes 12589056 | tf_op jit(solution)/shard_map/reduce_sum | solution.py:56
  87.1 7.6 %multiply_reduce_fusion = (f32[768]{0:T(1024)S(1)}, f32[768,4096]{1,0:T(8,128)}) fusion(bf16[768,128]{1,0:T(8,128)(2,1)S(1)} %reshape.179, bf16[4096,512]{1,0:T(8,128)(2,1)} %param.10), kind=kOutput, calls=%fused_computation.7 | convolution fusion | flops 811597056 | bytes 13831168 | tf_op jit(solution)/shard_map/dot_general | solution.py:51
  94.9 7.0 %fusion.7 = f32[768]{0:T(1024)S(1)} fusion(f32[768,4096]{1,0:T(8,128)} %get-tuple-element.16, f32[768]{0:T(1024)S(1)} %get-tuple-element.15), kind=kLoop, calls=%fused_computation.18 | loop fusion | flops 9436416 | bytes 12589056 | tf_op jit(solution)/shard_map/reduce_sum | solution.py:56
  102.1 7.5 %multiply_reduce_fusion.3 = (f32[768]{0:T(1024)S(1)}, f32[768,4096]{1,0:T(8,128)}) fusion(bf16[768,128]{1,0:T(8,128)(2,1)S(1)} %reshape.176, bf16[4096,512]{1,0:T(8,128)(2,1)} %param.10), kind=kOutput, calls=%fused_computation.10 | convolution fusion | flops 811597056 | bytes 13831168 | tf_op jit(solution)/shard_map/dot_general | solution.py:51
  109.8 6.8 %fusion.1 = f32[768]{0:T(1024)S(1)} fusion(f32[768,4096]{1,0:T(8,128)} %get-tuple-element.22, f32[768]{0:T(1024)S(1)} %get-tuple-element.21), kind=kLoop, calls=%fused_computation.12 | loop fusion | flops 9436416 | bytes 12589056 | tf_op jit(solution)/shard_map/reduce_sum | solution.py:56
  117.7 5.7 %all-to-all-start.2 = ((f32[16,1,192]{2,1,0:T(1,128)}), f32[16,1,192]{2,1,0:T(1,128)S(1)}, u32[]{:S(2)}, u32[]{:S(2)}) async-start(f32[16,1,192]{2,1,0:T(1,128)} %reshape.220), calls=%async_computation.2 | async-start | bytes 32768 | tf_op jit(solution)/shard_map/all_to_all | solution.py:70
  123.4 7.2 %fusion.46 = bf16[768,128]{1,0:T(8,128)(2,1)S(1)} fusion(bf16[4096,512]{1,0:T(8,128)(2,1)} %param.11, f32[768,4096]{1,0:T(8,128)} %get-tuple-element.20, f32[768]{0:T(1024)S(1)} %get-tuple-element.19, f32[768]{0:T(1024)S(1)} %fusion.3), kind=kOutput, calls=%fused_computation.45 | convolution fusion | flops 814940160 | bytes 13834240 | tf_op jit(solution)/shard_map/dot_general | solution.py:58
  130.7 7.6 %fusion.56 = bf16[768,128]{1,0:T(8,128)(2,1)S(1)} fusion(bf16[4096,512]{1,0:T(8,128)(2,1)S(1)} %copy-done.3, f32[768,4096]{1,0:T(8,128)} %get-tuple-element.18, f32[768]{0:T(1024)S(1)} %get-tuple-element.17, f32[768]{0:T(1024)S(1)} %fusion.5), kind=kOutput, calls=%fused_computation.47 | convolution fusion | flops 814940160 | bytes 13836288 | tf_op jit(solution)/shard_map/dot_general | solution.py:58
  138.4 2.1 %fusion.66 = bf16[768,128]{1,0:T(8,128)(2,1)S(1)} fusion(bf16[4096,512]{1,0:T(8,128)(2,1)S(1)} %copy-done.3, f32[768,4096]{1,0:T(8,128)S(1)} %bitcast.53, f32[768]{0:T(1024)S(1)} %get-tuple-element.15, f32[768]{0:T(1024)S(1)} %fusion.7), kind=kOutput, calls=%fused_computation.49 | convolution fusion | flops 814940160 | bytes 13836288 | tf_op jit(solution)/shard_map/dot_general | solution.py:58
  140.5 0.7 slice-done.5
  141.2 2.1 %fusion.36 = bf16[768,128]{1,0:T(8,128)(2,1)S(1)} fusion(bf16[4096,512]{1,0:T(8,128)(2,1)S(1)} %copy-done.3, f32[768,4096]{1,0:T(8,128)S(1)} %bitcast.55, f32[768]{0:T(1024)S(1)} %get-tuple-element.21, f32[768]{0:T(1024)S(1)} %fusion.1), kind=kOutput, calls=%fused_computation.43 | convolution fusion | flops 814940160 | bytes 13836288 | tf_op jit(solution)/shard_map/dot_general | solution.py:58
  144.6 6.0 %all-to-all-start.1 = ((f32[16,1,192]{2,1,0:T(1,128)}), f32[16,1,192]{2,1,0:T(1,128)S(1)}, u32[]{:S(2)}, u32[]{:S(2)}) async-start(f32[16,1,192]{2,1,0:T(1,128)} %reshape.218), calls=%async_computation.1 | async-start | bytes 32768 | tf_op jit(solution)/shard_map/all_to_all | solution.py:69
  150.6 1.4 pad_maximum_fusion
  152.0 5.1 %all-to-all-done.1 = f32[16,1,192]{2,1,0:T(1,128)S(1)} async-done(((f32[16,1,192]{2,1,0:T(1,128)}), f32[16,1,192]{2,1,0:T(1,128)S(1)}, u32[]{:S(2)}, u32[]{:S(2)}) %all-to-all-start.1) | async-done | bytes 12320 | tf_op jit(solution)/shard_map/all_to_all | solution.py:69
  157.1 3.8 %all-to-all-start.3 = ((bf16[16,3,4,2048]{3,2,1,0:T(4,128)(2,1)}), bf16[16,3,4,2048]{3,2,1,0:T(4,128)(2,1)S(1)}, u32[]{:S(2)}, u32[]{:S(2)}) async-start(bf16[16,3,4,2048]{3,2,1,0:T(4,128)(2,1)} %pad_maximum_fusion), calls=%async_computation.3 | async-start | bytes 1572864 | tf_op jit(solution)/shard_map/all_to_all | solution.py:68
  161.3 1.3 fusion.89
  167.3 12.1 %all-to-all-done.3 = bf16[16,3,4,2048]{3,2,1,0:T(4,128)(2,1)S(1)} async-done(((bf16[16,3,4,2048]{3,2,1,0:T(4,128)(2,1)}), bf16[16,3,4,2048]{3,2,1,0:T(4,128)(2,1)S(1)}, u32[]{:S(2)}, u32[]{:S(2)}) %all-to-all-start.3) | async-done | bytes 786464 | tf_op jit(solution)/shard_map/all_to_all | solution.py:68
  181.1 9.5 %convolution_convert_fusion.1 = bf16[32,4096]{1,0:T(8,128)(2,1)} fusion(bf16[2048,4096]{1,0:T(8,128)(2,1)} %all-gather.2.cloned.1.call-done, f32[4,8,16,128]{3,2,1,0:T(8,128)S(1)} %bitcast.57, f32[4,8,16,128]{3,2,1,0:T(8,128)S(1)} %bitcast.59, f32[32,2048]{1,0:T(8,128)S(1)} %reshape.182, f32[4,8,16,128]{3,2,1,0:T(8,128)S(1)} %bitcast.58), kind=kOutput, calls=%fused_computation.24 | convolution fusion | flops 537264128 | bytes 18087936 | tf_op jit(solution)/shard_map/dot_general | solution.py:107
  (83 shorter events, 13.3 us)
Async XLA Ops:
  6.5 174.3 %all-gather.2.cloned.1.call-start = ((), (), s32[]{:S(2)}) async-start(), calls=%async_computation.4 | async-start | bytes 17825792 | tf_op jit(solution)/shard_map/all_gather | solution.py:109
  117.7 26.9 %all-to-all-start.2 = ((f32[16,1,192]{2,1,0:T(1,128)}), f32[16,1,192]{2,1,0:T(1,128)S(1)}, u32[]{:S(2)}, u32[]{:S(2)}) async-start(f32[16,1,192]{2,1,0:T(1,128)} %reshape.220), calls=%async_computation.2 | async-start | bytes 32768 | tf_op jit(solution)/shard_map/all_to_all | solution.py:70
  123.4 7.3 %copy-start.3 = (bf16[4096,512]{1,0:T(8,128)(2,1)S(1)}, bf16[4096,512]{1,0:T(8,128)(2,1)}, u32[]{:S(2)}) copy-start(bf16[4096,512]{1,0:T(8,128)(2,1)} %param.11) | copy-start | bytes 12582916
  123.4 14.9 %slice-start = ((s8[12582912]{0:T(1024)(128)(4,1)}), s8[4194304]{0:T(1024)(128)(4,1)S(1)}, s32[]{:S(2)}) async-start(s8[12582912]{0:T(1024)(128)(4,1)} %bitcast.52), calls=%async_computation.5 | async-start | bytes 8388608
  123.4 14.9 %slice-start.1 = ((s8[12582912]{0:T(1024)(128)(4,1)}), s8[4194304]{0:T(1024)(128)(4,1)S(1)}, s32[]{:S(2)}) async-start(s8[12582912]{0:T(1024)(128)(4,1)} %bitcast.52), calls=%async_computation.6 | async-start | bytes 8388608
  130.6 7.7 %slice-start.2 = ((s8[12582912]{0:T(1024)(128)(4,1)}), s8[4194304]{0:T(1024)(128)(4,1)S(1)}, s32[]{:S(2)}) async-start(s8[12582912]{0:T(1024)(128)(4,1)} %bitcast.52), calls=%async_computation.7 | async-start | bytes 8388608
  130.6 9.8 %slice-start.3 = ((s8[12582912]{0:T(1024)(128)(4,1)}), s8[4194304]{0:T(1024)(128)(4,1)S(1)}, s32[]{:S(2)}) async-start(s8[12582912]{0:T(1024)(128)(4,1)} %bitcast.54), calls=%async_computation.8 | async-start | bytes 8388608
  130.7 9.8 %slice-start.4 = ((s8[12582912]{0:T(1024)(128)(4,1)}), s8[4194304]{0:T(1024)(128)(4,1)S(1)}, s32[]{:S(2)}) async-start(s8[12582912]{0:T(1024)(128)(4,1)} %bitcast.54), calls=%async_computation.9 | async-start | bytes 8388608
  138.3 2.9 %slice-start.5 = ((s8[12582912]{0:T(1024)(128)(4,1)}), s8[4194304]{0:T(1024)(128)(4,1)S(1)}, s32[]{:S(2)}) async-start(s8[12582912]{0:T(1024)(128)(4,1)} %bitcast.54), calls=%async_computation.10 | async-start | bytes 8388608
  141.2 19.7 %copy-start = (bf16[32,2048]{1,0:T(8,128)(2,1)S(1)}, bf16[32,2048]{1,0:T(8,128)(2,1)}, u32[]{:S(2)}) copy-start(bf16[32,2048]{1,0:T(8,128)(2,1)} %param.7) | copy-start | bytes 393220
  141.2 20.0 %copy-start.1 = (bf16[32,512]{1,0:T(8,128)(2,1)S(1)}, bf16[32,512]{1,0:T(8,128)(2,1)}, u32[]{:S(2)}) copy-start(bf16[32,512]{1,0:T(8,128)(2,1)} %param.8) | copy-start | bytes 98308
  141.2 20.0 %copy-start.2 = (bf16[32,512]{1,0:T(8,128)(2,1)S(1)}, bf16[32,512]{1,0:T(8,128)(2,1)}, u32[]{:S(2)}) copy-start(bf16[32,512]{1,0:T(8,128)(2,1)} %param.9) | copy-start | bytes 98308
  144.6 12.5 %all-to-all-start.1 = ((f32[16,1,192]{2,1,0:T(1,128)}), f32[16,1,192]{2,1,0:T(1,128)S(1)}, u32[]{:S(2)}, u32[]{:S(2)}) async-start(f32[16,1,192]{2,1,0:T(1,128)} %reshape.218), calls=%async_computation.1 | async-start | bytes 32768 | tf_op jit(solution)/shard_map/all_to_all | solution.py:69
  157.1 22.3 %all-to-all-start.3 = ((bf16[16,3,4,2048]{3,2,1,0:T(4,128)(2,1)}), bf16[16,3,4,2048]{3,2,1,0:T(4,128)(2,1)S(1)}, u32[]{:S(2)}, u32[]{:S(2)}) async-start(bf16[16,3,4,2048]{3,2,1,0:T(4,128)(2,1)} %pad_maximum_fusion), calls=%async_computation.3 | async-start | bytes 1572864 | tf_op jit(solution)/shard_map/all_to_all | solution.py:68
Sparse Core Ops, SparseCore 0:
  9.5 148.0 all-gather.1
where the time goes:
time: 198 us; the launch traced here: 197 us
  matrix products  60.7 us (31%)
  blocking collectives  44.6 us (23%)
  other arithmetic  34.4 us (17%)
  waiting for transfers between devices  18 us (9%)
  starting transfers between devices  15.5 us (8%)
  between operations  13.9 us (7%)
  local copies, waits for them, and re-layouts  10.4 us (5%)
    all_to_all x1, blocking collectives, shards(): lax.all_to_all(outgoing, 'seq', split_axis=0, concat_axis=0, tiled=True)  44.6 us
    dot_general x4, matrix products, shards(): lax.dot_general(asked, cached_keys, (((1,), (1,)), ((), ())), preferred_e...  30.2 us
    reduce_sum x4, other arithmetic, shards(): summed = jnp.sum(weights, axis=1, keepdims=True)  28.8 us
    dot_general x4, matrix products, shards(): jnp.dot(weights.astype(jnp.bfloat16), cached_values, preferred_element_ty...  19 us
    all_to_all x1, waiting for transfers between devices, shards(): lax.all_to_all(partial_out, 'seq', split_axis=0, concat_axis=0, tiled=True)  12.1 us
    dot_general x1, matrix products, shards(): jnp.dot(attended, lax.all_gather(out_weight, 'seq', axis=1, tiled=True),...  9.49 us
    all_to_all x1, starting transfers between devices, shards(): lax.all_to_all(maxima_all, 'seq', split_axis=0, concat_axis=0, tiled=True)  5.99 us
    all_to_all x1, starting transfers between devices, shards(): lax.all_to_all(totals_all, 'seq', split_axis=0, concat_axis=0, tiled=True)  5.68 us
  transfers between devices with their start and end apart: 4, of which 2 were waited for; matrix products, arithmetic and copies ran while one was open for 48% of the time, Pallas kernels for 0%

commit v1 on v0

v1 whole, which is shorter than its diff:
```python
import functools
import math

import jax
import jax.numpy as jnp
from jax import lax
from jax.experimental import pallas as pl
from jax.experimental.pallas import tpu as pltpu
from jax.sharding import PartitionSpec as P

HQ = 16
KVH = 4
HD = 128
PER = HQ // KVH
SCALE = 1.0 / math.sqrt(HD)
LOG2E = math.log2(math.e)


def flash_rows(q, k_ref, v_ref, chunk):
    nt = (((1,), (1,)), ((), ()))
    count = k_ref.shape[0] // chunk
    score = lambda c: lax.dot_general(
        q, k_ref[c * chunk : (c + 1) * chunk, :], nt, preferred_element_type=jnp.float32
    )
    high = total = acc = None
    nxt = score(0)
    for c in range(count):
        s = nxt
        if c + 1 < count:
            nxt = score(c + 1)
        m = jnp.max(s, axis=1, keepdims=True)
        new = m if c == 0 else jnp.maximum(high, m)
        w = jnp.exp2((s - new) * (SCALE * LOG2E))
        t = jnp.sum(w, axis=1, keepdims=True)
        o = jnp.dot(
            w.astype(jnp.bfloat16),
            v_ref[c * chunk : (c + 1) * chunk, :],
            preferred_element_type=jnp.float32,
        )
        if c == 0:
            total, acc = t, o
        else:
            fix = jnp.exp2((high - new) * (SCALE * LOG2E))
            total = total * fix + t
            acc = acc * fix + o
        high = new
    return acc / total, high * SCALE, total


def page_kernel(block, chunk, q_ref, k_ref, v_ref, out_ref, stat_ref):
    @pl.loop(0, q_ref.shape[1] // block)
    def _(i):
        rows = pl.ds(pl.multiple_of(i * block, block), block)
        out, high, total = flash_rows(q_ref[0, rows, :], k_ref, v_ref, chunk)
        out_ref[0, rows, :] = out.astype(out_ref.dtype)
        stat_ref[0, rows, 0:1] = high
        stat_ref[0, rows, 1:2] = total


def page_attention(q, keys, values):
    rows = q.shape[1]
    page = keys.shape[0]
    block = next(b for b in (256, 128, 64, 16) if rows % b == 0)
    chunk = next(c for c in (1024, 512, page) if page % c == 0)
    return pl.pallas_call(
        functools.partial(page_kernel, block, chunk),
        grid=(KVH,),
        in_specs=[
            pl.BlockSpec((1, rows, HD), lambda g: (g, 0, 0)),
            pl.BlockSpec((page, HD), lambda g: (0, g)),
            pl.BlockSpec((page, HD), lambda g: (0, g)),
        ],
        out_specs=[
            pl.BlockSpec((1, rows, HD), lambda g: (g, 0, 0)),
            pl.BlockSpec((1, rows, 2), lambda g: (g, 0, 0)),
        ],
        out_shape=[
            jax.ShapeDtypeStruct((KVH, rows, HD), jnp.bfloat16),
            jax.ShapeDtypeStruct((KVH, rows, 2), jnp.float32),
        ],
        compiler_params=pltpu.CompilerParams(vmem_limit_bytes=40 * 1024 * 1024),
    )(q, keys, values)


def shards(queries, new_keys, new_values, keys, values, page_list, out_weight):
    members = lax.axis_size("seq")
    tiles, width = page_list.shape
    row_total, features = queries.shape
    rows = row_total // tiles
    unit = rows * PER
    capacity = max(1, 2 * tiles * width // members)
    slots = members * capacity
    ids = jnp.arange(tiles)
    before = ids[None, :] < ids[:, None]
    matches = page_list[:, :, None, None] == page_list[None, None, :, :]
    ranking = jnp.sum(matches & before[:, None, :, None], axis=(2, 3))
    slot_index = page_list * capacity + ranking
    placing = jnp.any(
        slot_index[:, :, None] == jnp.arange(slots, dtype=jnp.int32)[None, None, :], axis=1
    ).astype(jnp.bfloat16)
    asked = queries.reshape(tiles, rows, KVH, PER, HD).transpose(0, 2, 1, 3, 4)
    asked = asked.reshape(tiles, KVH, unit, HD)
    outgoing = lax.dot_general(
        placing,
        asked.reshape(tiles, -1),
        (((0,), (0,)), ((), ())),
        preferred_element_type=jnp.float32,
    ).astype(jnp.bfloat16)
    outgoing = outgoing.reshape(members, capacity, KVH, unit, HD)
    incoming = lax.all_to_all(outgoing, "seq", split_axis=0, concat_axis=0, tiled=True)
    incoming = incoming.transpose(2, 0, 1, 3, 4).reshape(KVH, slots * unit, HD)
    out, stat = page_attention(incoming, keys, values)
    out = out.reshape(KVH, members, capacity, unit, HD).transpose(1, 2, 0, 3, 4)
    stat = stat.reshape(KVH, members, capacity, unit, 2).transpose(1, 2, 0, 3, 4)
    stat = stat.reshape(members, capacity, KVH * unit * 2)
    got = lax.all_to_all(out, "seq", split_axis=0, concat_axis=0, tiled=True)
    got_stat = lax.all_to_all(stat, "seq", split_axis=0, concat_axis=0, tiled=True)
    a = asked.reshape(tiles, KVH, rows, PER, HD).astype(jnp.float32)
    nk = new_keys.reshape(tiles, rows, KVH, HD).transpose(0, 2, 1, 3).astype(jnp.float32)
    nv = new_values.reshape(tiles, rows, KVH, HD).transpose(0, 2, 1, 3).astype(jnp.float32)
    own_s = jnp.sum(a[:, :, :, :, None, :] * nk[:, :, None, None, :, :], axis=-1) * SCALE
    causal = jnp.arange(rows)[:, None] >= jnp.arange(rows)[None, :]
    own_s = jnp.where(causal[None, None, :, None, :], own_s, -jnp.inf)
    own_max = jnp.max(own_s, axis=-1)
    own_w = jnp.exp(own_s - own_max[..., None])
    own_total = jnp.sum(own_w, axis=-1)
    own_w = own_w.astype(jnp.bfloat16).astype(jnp.float32)
    own_sum = jnp.sum(own_w[..., None] * nv[:, :, None, None, :, :], axis=4)

    pick = slot_index[:, :, None] == jnp.arange(slots, dtype=jnp.int32)
    chosen = lax.dot_general(
        pick.reshape(tiles * width, slots).astype(jnp.bfloat16),
        got.reshape(slots, KVH * unit * HD),
        (((1,), (0,)), ((), ())),
        preferred_element_type=jnp.float32,
    ).reshape(tiles, width, KVH, rows, PER, HD)
    got_stat = got_stat.reshape(slots, KVH, rows, PER, 2)
    chosen_stat = jnp.sum(
        jnp.where(pick[..., None], got_stat.reshape(slots, -1)[None, None], 0.0), axis=2
    ).reshape(tiles, width, KVH, rows, PER, 2)
    chosen_max = chosen_stat[..., 0]
    chosen_total = chosen_stat[..., 1]
    top = jnp.maximum(own_max, jnp.max(chosen_max, axis=1))
    own_exp = jnp.exp(own_max - top)
    factor = chosen_total * jnp.exp(chosen_max - top[:, None])
    denom = own_exp * own_total + jnp.sum(factor, axis=1)
    numer = own_exp[..., None] * own_sum + jnp.sum(factor[..., None] * chosen, axis=1)
    attended = (numer / denom[..., None]).astype(jnp.bfloat16)
    attended = attended.transpose(0, 2, 1, 3, 4).reshape(row_total, features)
    everyone = lax.all_gather(attended, "seq", axis=0, tiled=True)
    columns = jnp.dot(everyone, out_weight, preferred_element_type=jnp.float32)
    columns = columns.astype(jnp.bfloat16).reshape(members, row_total, -1)
    mine = lax.all_to_all(columns, "seq", split_axis=0, concat_axis=0, tiled=True)
    return mine.transpose(1, 0, 2).reshape(row_total, -1)


def solution(mesh):
    rows = P(("groups", "seq"), None)
    return jax.shard_map(
        shards,
        mesh=mesh,
        in_specs=(rows, rows, rows, rows, rows, rows, P(None, "seq")),
        out_specs=rows,
        check_vma=False,
    )
```

time: 198 us -> 168 us (0.85)
  waiting for transfers between devices: 18 us -> 82.3 us
  matrix products: 60.7 us -> 3.31 us
  blocking collectives: 44.6 us -> 13.3 us
  other arithmetic: 34.4 us -> 3.68 us
  Pallas kernels: 0 us -> 19.6 us
  local copies, waits for them, and re-layouts: 10.4 us -> 14.8 us
    dot_general x12 -> x3, matrix products: 60.7 us -> 3.31 us  [the longest x1 2.3 us: shards(): columns = jnp.dot(everyone, out_weight, preferred_element_type=jnp.float32)]
    all_gather x1, waiting for transfers between devices: 0.02 us -> 42.3 us  [shards(): everyone = lax.all_gather(attended, 'seq', axis=0, tiled=True)]
    all_to_all x1, blocking collectives: 44.6 us -> 13.3 us  [shards(): lax.all_to_all(columns, 'seq', split_axis=0, concat_axis=0, tiled=True)]
    reduce_sum x7 -> x5, other arithmetic: 29.4 us -> 1.31 us  [the longest x1 0.45 us: shards(): jnp.sum(a[:, :, :, :, None, :] * nk[:, :, None, None, :, :], axis=-1)]
    all_to_all x3, waiting for transfers between devices: 17.2 us -> 40 us  [the longest x1 18.2 us: shards(): lax.all_to_all(outgoing, 'seq', split_axis=0, concat_axis=0, tiled=True)]
    pallas_call x0 -> x1, Pallas kernels: none -> 19.6 us  [page_attention(): pl.pallas_call(functools.partial(page_kernel, block, chunk), grid=(KVH,),...]
    reshape x14 -> x8, local copies, waits for them, and re-layouts: 3.14 us -> 8.41 us  [the longest x1 1.88 us: shards(): stat.reshape(KVH, members, capacity, unit, 2).transpose(1, 2, 0, 3, 4)]
    unnamed x24 -> x9, local copies, waits for them, and re-layouts: 2.44 us -> 4.56 us
  transfers between devices with their start and end apart: 4 -> 4, of which waited for: 2 -> 4; matrix products, arithmetic and copies ran while one was open for 48% -> 2% of each run, Pallas kernels for 0% -> 0%
where the time goes in v1:
time: 168 us; the launch traced here: 167 us
  waiting for transfers between devices  82.3 us (49%)
  Pallas kernels  19.6 us (12%)
  starting transfers between devices  16.5 us (10%)
  local copies, waits for them, and re-layouts  14.8 us (9%)
  between operations  13.6 us (8%)
  blocking collectives  13.3 us (8%)
  other arithmetic  3.68 us (2%)
  matrix products  3.31 us (2%)
    all_gather x1, waiting for transfers between devices, shards(): everyone = lax.all_gather(attended, 'seq', axis=0, tiled=True)  42.3 us
    pallas_call x1, Pallas kernels, page_attention(): pl.pallas_call(functools.partial(page_kernel, block, chunk), grid=(KVH,),...  19.6 us
    all_to_all x1, waiting for transfers between devices, shards(): lax.all_to_all(outgoing, 'seq', split_axis=0, concat_axis=0, tiled=True)  18.2 us
    all_to_all x1, waiting for transfers between devices, shards(): got = lax.all_to_all(out, 'seq', split_axis=0, concat_axis=0, tiled=True)  17.1 us
    all_to_all x1, blocking collectives, shards(): lax.all_to_all(columns, 'seq', split_axis=0, concat_axis=0, tiled=True)  13.3 us
    all_to_all x1, starting transfers between devices, shards(): lax.all_to_all(outgoing, 'seq', split_axis=0, concat_axis=0, tiled=True)  7.39 us
    all_to_all x1, starting transfers between devices, shards(): lax.all_to_all(stat, 'seq', split_axis=0, concat_axis=0, tiled=True)  5.48 us
    all_to_all x1, waiting for transfers between devices, shards(): lax.all_to_all(stat, 'seq', split_axis=0, concat_axis=0, tiled=True)  4.68 us
  transfers between devices with their start and end apart: 4, of which 4 were waited for; matrix products, arithmetic and copies ran while one was open for 2% of the time, Pallas kernels for 0%

profile of v1, /device:TPU:0, one launch (start us, length us, event | category | flops | bytes accessed | tf_op | source)
XLA Modules:
  0.0 167.2 jit_solution(14840818997115776784)
XLA Ops:
  6.5 1.0 convert_reduce_fusion
  7.5 0.7 multiply_add_fusion
  8.3 1.0 reshape.129
  10.0 1.0 copy.108
  11.0 7.4 %all-to-all-start = ((bf16[16,3,4,16,128]{4,3,1,2,0:T(8,128)(2,1)}), bf16[16,3,4,16,128]{4,3,1,2,0:T(8,128)(2,1)S(1)}, u32[]{:S(2)}, u32[]{:S(2)}) async-start(bf16[16,3,4,16,128]{4,3,1,2,0:T(8,128)(2,1)} %copy.108), calls=%async_computation | async-start | bytes 1572864 | tf_op jit(solution)/shard_map/all_to_all | solution.py:110
  19.0 18.2 %all-to-all-done = bf16[16,3,4,16,128]{4,3,1,2,0:T(8,128)(2,1)S(1)} async-done(((bf16[16,3,4,16,128]{4,3,1,2,0:T(8,128)(2,1)}), bf16[16,3,4,16,128]{4,3,1,2,0:T(8,128)(2,1)S(1)}, u32[]{:S(2)}, u32[]{:S(2)}) %all-to-all-start) | async-done | bytes 786464 | tf_op jit(solution)/shard_map/all_to_all | solution.py:110
  37.2 2.2 %copy-done.1 = bf16[4096,512]{1,0:T(8,128)(2,1)S(1)} copy-done((bf16[4096,512]{1,0:T(8,128)(2,1)S(1)}, bf16[4096,512]{1,0:T(8,128)(2,1)}, u32[]{:S(2)}) %copy-start.1) | copy-done | bytes 4194328
  39.4 2.2 %copy-done.2 = bf16[4096,512]{1,0:T(8,128)(2,1)S(1)} copy-done((bf16[4096,512]{1,0:T(8,128)(2,1)S(1)}, bf16[4096,512]{1,0:T(8,128)(2,1)}, u32[]{:S(2)}) %copy-start.2) | copy-done | bytes 4194328
  41.6 19.6 %shard_map.73 = (bf16[4,768,128]{2,1,0:T(8,128)(2,1)S(1)}, f32[4,768,2]{2,1,0:T(8,128)S(1)}) custom-call(bf16[4,768,128]{2,1,0:T(8,128)(2,1)S(1)} %bitcast.73, bf16[4096,512]{1,0:T(8,128)(2,1)S(1)} %copy-done.1, bf16[4096,512]{1,0:T(8,128)(2,1)S(1)} %copy-done.2), custom_call_target="tpu_custom_call" | custom-call | tf_op jit(solution)/shard_map/pallas_call | solution.py:65
  61.2 1.9 %copy.110 = f32[4,16,3,16,2]{1,4,3,0,2:T(2,128)} copy(f32[4,16,3,16,2]{4,3,2,1,0:T(8,128)S(1)} %bitcast.74) | data formatting | bytes 49152 | tf_op jit(solution)/shard_map/reshape | solution.py:114
  63.1 1.6 copy.111
  64.7 5.5 %all-to-all-start.1 = ((f32[16,3,128]{2,1,0:T(4,128)}), f32[16,3,128]{2,1,0:T(4,128)S(1)}, u32[]{:S(2)}, u32[]{:S(2)}) async-start(f32[16,3,128]{2,1,0:T(4,128)} %copy.111), calls=%async_computation.1 | async-start | bytes 65536 | tf_op jit(solution)/shard_map/all_to_all | solution.py:117
  70.3 0.8 reshape.141
  71.1 1.1 copy.131
  72.2 4.7 %all-to-all-done.1 = f32[16,3,128]{2,1,0:T(4,128)S(1)} async-done(((f32[16,3,128]{2,1,0:T(4,128)}), f32[16,3,128]{2,1,0:T(4,128)S(1)}, u32[]{:S(2)}, u32[]{:S(2)}) %all-to-all-start.1) | async-done | bytes 24608 | tf_op jit(solution)/shard_map/all_to_all | solution.py:117
  76.9 3.6 %all-to-all-start.2 = ((bf16[16,3,4,16,128]{4,3,2,1,0:T(8,128)(2,1)}), bf16[16,3,4,16,128]{4,3,2,1,0:T(8,128)(2,1)S(1)}, u32[]{:S(2)}, u32[]{:S(2)}) async-start(bf16[16,3,4,16,128]{4,3,2,1,0:T(8,128)(2,1)} %bitcast.72), calls=%async_computation.2 | async-start | bytes 1572864 | tf_op jit(solution)/shard_map/all_to_all | solution.py:116
  82.0 17.1 %all-to-all-done.2 = bf16[16,3,4,16,128]{4,3,2,1,0:T(8,128)(2,1)S(1)} async-done(((bf16[16,3,4,16,128]{4,3,2,1,0:T(8,128)(2,1)}), bf16[16,3,4,16,128]{4,3,2,1,0:T(8,128)(2,1)S(1)}, u32[]{:S(2)}, u32[]{:S(2)}) %all-to-all-start.2) | async-done | bytes 786464 | tf_op jit(solution)/shard_map/all_to_all | solution.py:116
  99.5 0.6 dot_general.15
  100.1 0.6 fusion.1
  100.9 0.7 reshape.137
  101.7 42.3 %all-gather.2.cloned.1.call-done = bf16[512,2048]{1,0:T(8,128)(2,1)} async-done(((bf16[32,2048]{1,0:T(8,128)(2,1)}), bf16[512,2048]{1,0:T(8,128)(2,1)}) %all-gather.2.cloned.1.call-update) | async-done | bytes 2097168 | tf_op jit(solution)/shard_map/all_gather | solution.py:150
  144.0 2.3 %convolution_convert_fusion.1 = bf16[512,256]{1,0:T(8,128)(2,1)S(1)} fusion(bf16[512,2048]{1,0:T(8,128)(2,1)} %all-gather.2.cloned.1.call-done, bf16[2048,256]{1,0:T(8,128)(2,1)S(1)} %copy-done), kind=kOutput, calls=%fused_computation.4 | convolution fusion | flops 537001984 | bytes 3407872 | tf_op jit(solution)/shard_map/dot_general | solution.py:151
  146.3 13.3 %all_to_all.20 = bf16[16,32,256]{2,1,0:T(8,128)(2,1)S(1)} all-to-all(bf16[16,32,256]{2,1,0:T(8,128)(2,1)S(1)} %bitcast.88), channel_id=1, replica_groups=mesh['groups'=2,'seq'=16] {'seq'}, dimensions={0} | all-to-all | bytes 524288 | tf_op jit(solution)/shard_map/all_to_all | solution.py:153
  159.6 0.7 copy.122
  (35 shorter events, 3.5 us)
Async XLA Ops:
  6.5 137.5 %copy-start = (bf16[2048,256]{1,0:T(8,128)(2,1)S(1)}, bf16[2048,256]{1,0:T(8,128)(2,1)}, u32[]{:S(2)}) copy-start(bf16[2048,256]{1,0:T(8,128)(2,1)} %param.13) | copy-start | bytes 3145732
  9.8 8.6 %copy-start.3 = (bf16[32,512]{1,0:T(8,128)(2,1)S(1)}, bf16[32,512]{1,0:T(8,128)(2,1)}, u32[]{:S(2)}) copy-start(bf16[32,512]{1,0:T(8,128)(2,1)} %param.8) | copy-start | bytes 98308
  11.0 26.1 %all-to-all-start = ((bf16[16,3,4,16,128]{4,3,1,2,0:T(8,128)(2,1)}), bf16[16,3,4,16,128]{4,3,1,2,0:T(8,128)(2,1)S(1)}, u32[]{:S(2)}, u32[]{:S(2)}) async-start(bf16[16,3,4,16,128]{4,3,1,2,0:T(8,128)(2,1)} %copy.108), calls=%async_computation | async-start | bytes 1572864 | tf_op jit(solution)/shard_map/all_to_all | solution.py:110
  37.2 2.2 %copy-start.1 = (bf16[4096,512]{1,0:T(8,128)(2,1)S(1)}, bf16[4096,512]{1,0:T(8,128)(2,1)}, u32[]{:S(2)}) copy-start(bf16[4096,512]{1,0:T(8,128)(2,1)} %k_ref.1) | copy-start | bytes 12582916
  39.4 2.2 %copy-start.2 = (bf16[4096,512]{1,0:T(8,128)(2,1)S(1)}, bf16[4096,512]{1,0:T(8,128)(2,1)}, u32[]{:S(2)}) copy-start(bf16[4096,512]{1,0:T(8,128)(2,1)} %v_ref.1) | copy-start | bytes 12582916
  64.7 12.1 %all-to-all-start.1 = ((f32[16,3,128]{2,1,0:T(4,128)}), f32[16,3,128]{2,1,0:T(4,128)S(1)}, u32[]{:S(2)}, u32[]{:S(2)}) async-start(f32[16,3,128]{2,1,0:T(4,128)} %copy.111), calls=%async_computation.1 | async-start | bytes 65536 | tf_op jit(solution)/shard_map/all_to_all | solution.py:117
  76.9 22.3 %all-to-all-start.2 = ((bf16[16,3,4,16,128]{4,3,2,1,0:T(8,128)(2,1)}), bf16[16,3,4,16,128]{4,3,2,1,0:T(8,128)(2,1)S(1)}, u32[]{:S(2)}, u32[]{:S(2)}) async-start(bf16[16,3,4,16,128]{4,3,2,1,0:T(8,128)(2,1)} %bitcast.72), calls=%async_computation.2 | async-start | bytes 1572864 | tf_op jit(solution)/shard_map/all_to_all | solution.py:116
  80.5 63.5 %all-gather.2.cloned.1.call-start = ((), (), s32[]{:S(2)}) async-start(), calls=%async_computation.4 | async-start | bytes 2228224 | tf_op jit(solution)/shard_map/all_gather | solution.py:150
Sparse Core Ops, SparseCore 0:
  101.8 42.1 all-gather.1

commit v2 on v1

--- a/solution.py
+++ b/solution.py
@@ -80,6 +80,154 @@
         ],
         compiler_params=pltpu.CompilerParams(vmem_limit_bytes=40 * 1024 * 1024),
     )(q, keys, values)
+
+
+def project_kernel(n, att_ref, w_ref, out_ref, held, result, got, r_send, r_recv, l_send, l_recv, s_send, s_recv, p_send, p_recv):
+    me = lax.axis_index("seq")
+    rows = att_ref.shape[0]
+    wide = w_ref.shape[1]
+    chips = n // 2
+    core = lax.rem(me, 2)
+    chip = me // 2
+    half = (chips + 1) // 2
+    place = jnp.where(lax.rem(chip, 2) == 0, chip // 2, chips - 1 - chip // 2)
+
+    def chip_at(p):
+        p = lax.rem(p + 2 * chips, chips)
+        return jnp.where(p < half, 2 * p, 2 * (chips - 1 - p) + 1)
+
+    sibling = chip * 2 + (1 - core)
+    right = chip_at(place + 1) * 2 + core
+    left = chip_at(place - 1) * 2 + core
+
+    barrier = pltpu.get_barrier_semaphore()
+
+    @pl.loop(0, n - 1)
+    def _(i):
+        pl.semaphore_signal(
+            barrier, inc=1, device_id={"seq": lax.rem(me + 1 + i, n)},
+            device_id_type=pl.DeviceIdType.MESH,
+        )
+
+    held[pl.ds(pl.multiple_of(me * rows, rows), rows), :] = att_ref[...]
+    pl.semaphore_wait(barrier, n - 1)
+
+    def block(d):
+        return held.at[pl.ds(pl.multiple_of(d * rows, rows), rows), :]
+
+    def move(d, to, send, recv):
+        return pltpu.make_async_remote_copy(
+            src_ref=block(d), dst_ref=block(d), send_sem=send, recv_sem=recv,
+            device_id={"seq": to}, device_id_type=pl.DeviceIdType.MESH,
+        )
+
+    def give(d, slot):
+        return pltpu.make_async_remote_copy(
+            src_ref=result.at[pl.ds(pl.multiple_of(d * rows, rows), rows), :],
+            dst_ref=got.at[pl.ds(pl.multiple_of(me * rows, rows), rows), :],
+            send_sem=p_send.at[slot], recv_sem=p_recv.at[me],
+            device_id={"seq": d}, device_id_type=pl.DeviceIdType.MESH,
+        )
+
+    rights, lefts = chips // 2, (chips - 1) // 2
+    started = []
+
+    def project(c):
+        return jnp.dot(
+            held[pl.ds(pl.multiple_of(c * 2 * rows, 2 * rows), 2 * rows), :], w_ref[...],
+            preferred_element_type=jnp.float32,
+        ).astype(jnp.bfloat16)
+
+    def finish(k, c):
+        move(c * 2 + (1 - core), sibling, s_send.at[k], s_recv.at[k]).wait_recv()
+        result[pl.ds(pl.multiple_of(c * 2 * rows, 2 * rows), 2 * rows), :] = project(c)
+        if k == 0:
+            mine = result[pl.ds(pl.multiple_of(me * rows, rows), rows), :]
+            got[pl.ds(pl.multiple_of(me * rows, rows), rows), :] = mine
+            sent = [give(sibling, 0)]
+        else:
+            sent = [give(c * 2, 2 * k), give(c * 2 + 1, 2 * k + 1)]
+        for copy in sent:
+            copy.start()
+        started.extend(sent)
+
+    def launch(copy):
+        copy.start()
+        started.append(copy)
+
+    def step_right(s):
+        launch(move(chip_at(place - s) * 2 + core, right, r_send.at[s], r_recv.at[s]))
+
+    def step_left(s):
+        launch(move(chip_at(place + s) * 2 + core, left, l_send.at[s], l_recv.at[s]))
+
+    step_right(0)
+    if lefts:
+        step_left(0)
+    launch(move(me, sibling, s_send.at[0], s_recv.at[0]))
+    waiting = [(0, chip)]
+    k = 1
+    for s in range(rights):
+        c = chip_at(place - 1 - s)
+        move(c * 2 + core, right, r_send.at[s], r_recv.at[s]).wait_recv()
+        if s + 1 < rights:
+            step_right(s + 1)
+        launch(move(c * 2 + core, sibling, s_send.at[k], s_recv.at[k]))
+        now = [(k, c)]
+        k += 1
+        if s < lefts:
+            c = chip_at(place + 1 + s)
+            move(c * 2 + core, left, l_send.at[s], l_recv.at[s]).wait_recv()
+            if s + 1 < lefts:
+                step_left(s + 1)
+            launch(move(c * 2 + core, sibling, s_send.at[k], s_recv.at[k]))
+            now.append((k, c))
+            k += 1
+        for job in waiting:
+            finish(*job)
+        waiting = now
+    for job in waiting:
+        finish(*job)
+    for copy in started:
+        copy.wait_send()
+
+    @pl.loop(0, n - 1)
+    def _(i):
+        d = lax.rem(me + 1 + i, n)
+        pltpu.make_async_remote_copy(
+            src_ref=result.at[pl.ds(0, rows), :],
+            dst_ref=got.at[pl.ds(pl.multiple_of(d * rows, rows), rows), :],
+            send_sem=p_send.at[1], recv_sem=p_recv.at[d],
+            device_id={"seq": d}, device_id_type=pl.DeviceIdType.MESH,
+        ).wait_recv()
+
+    for d in range(n):
+        out_ref[:, d * wide : (d + 1) * wide] = got[d * rows : (d + 1) * rows, :]
+
+
+def project(attended, out_weight):
+    n = lax.axis_size("seq")
+    rows, features = attended.shape
+    wide = out_weight.shape[1]
+    chips = n // 2
+    vmem = pl.BlockSpec(memory_space=pltpu.VMEM)
+    dma = pltpu.SemaphoreType.DMA
+    return pl.pallas_call(
+        functools.partial(project_kernel, n),
+        out_shape=jax.ShapeDtypeStruct((rows, n * wide), jnp.bfloat16),
+        in_specs=[vmem, vmem],
+        out_specs=vmem,
+        scratch_shapes=[
+            pltpu.VMEM((n * rows, features), jnp.bfloat16),
+            pltpu.VMEM((n * rows, wide), jnp.bfloat16),
+            pltpu.VMEM((n * rows, wide), jnp.bfloat16),
+            dma((chips,)), dma((chips,)), dma((chips,)), dma((chips,)),
+            dma((chips,)), dma((chips,)), dma((n,)), dma((n,)),
+        ],
+        compiler_params=pltpu.CompilerParams(
+            collective_id=0, has_side_effects=True, vmem_limit_bytes=40 * 1024 * 1024
+        ),
+    )(attended, out_weight)
 
 
 def shards(queries, new_keys, new_values, keys, values, page_list, out_weight):
@@ -147,11 +295,7 @@
     numer = own_exp[..., None] * own_sum + jnp.sum(factor[..., None] * chosen, axis=1)
     attended = (numer / denom[..., None]).astype(jnp.bfloat16)
     attended = attended.transpose(0, 2, 1, 3, 4).reshape(row_total, features)
-    everyone = lax.all_gather(attended, "seq", axis=0, tiled=True)
-    columns = jnp.dot(everyone, out_weight, preferred_element_type=jnp.float32)
-    columns = columns.astype(jnp.bfloat16).reshape(members, row_total, -1)
-    mine = lax.all_to_all(columns, "seq", split_axis=0, concat_axis=0, tiled=True)
-    return mine.transpose(1, 0, 2).reshape(row_total, -1)
+    return project(attended, out_weight)
 
 
 def solution(mesh):

time: 168 us -> 122 us (0.73)
  waiting for transfers between devices: 82.3 us -> 40.8 us
  Pallas kernels: 19.6 us -> 47.3 us
  between operations: 13.6 us -> 0.26 us
  blocking collectives: 13.3 us -> 0 us
  local copies, waits for them, and re-layouts: 14.8 us -> 11.9 us
  matrix products: 3.31 us -> 1.01 us
    all_gather x1 -> x0, waiting for transfers between devices: 42.3 us -> none  [shards(): everyone = lax.all_gather(attended, 'seq', axis=0, tiled=True)]
    pallas_call x0 -> x1, Pallas kernels: none -> 27.7 us  [project(): pl.pallas_call(functools.partial(project_kernel, n), out_shape=jax.ShapeD...]
    all_to_all x1 -> x0, blocking collectives: 13.3 us -> none  [shards(): lax.all_to_all(columns, 'seq', split_axis=0, concat_axis=0, tiled=True)]
    dot_general x1 -> x0, matrix products: 2.3 us -> none  [shards(): columns = jnp.dot(everyone, out_weight, preferred_element_type=jnp.float32)]
    unnamed x9 -> x12, local copies, waits for them, and re-layouts: 4.56 us -> 5.27 us
  transfers between devices with their start and end apart: 4 -> 3, of which waited for: 4 -> 3; matrix products, arithmetic and copies ran while one was open for 2% -> 3% of each run, Pallas kernels for 0% -> 0%
where the time goes in v2:
time: 122 us; the launch traced here: 121 us
  Pallas kernels  47.3 us (39%)
  waiting for transfers between devices  40.8 us (33%)
  starting transfers between devices  16.5 us (14%)
  local copies, waits for them, and re-layouts  11.9 us (10%)
  other arithmetic  3.64 us (3%)
    pallas_call x1, Pallas kernels, project(): pl.pallas_call(functools.partial(project_kernel, n), out_shape=jax.ShapeD...  27.7 us
    pallas_call x1, Pallas kernels, page_attention(): pl.pallas_call(functools.partial(page_kernel, block, chunk), grid=(KVH,),...  19.6 us
    all_to_all x1, waiting for transfers between devices, shards(): lax.all_to_all(outgoing, 'seq', split_axis=0, concat_axis=0, tiled=True)  18.2 us
    all_to_all x1, waiting for transfers between devices, shards(): got = lax.all_to_all(out, 'seq', split_axis=0, concat_axis=0, tiled=True)  17.1 us
    all_to_all x1, starting transfers between devices, shards(): lax.all_to_all(outgoing, 'seq', split_axis=0, concat_axis=0, tiled=True)  7.39 us
    all_to_all x1, starting transfers between devices, shards(): lax.all_to_all(stat, 'seq', split_axis=0, concat_axis=0, tiled=True)  5.48 us
    all_to_all x1, waiting for transfers between devices, shards(): lax.all_to_all(stat, 'seq', split_axis=0, concat_axis=0, tiled=True)  5.42 us
    unnamed x12, local copies, waits for them, and re-layouts  5.27 us
  transfers between devices with their start and end apart: 3, of which 3 were waited for; matrix products, arithmetic and copies ran while one was open for 3% of the time, Pallas kernels for 0%

profile of v2, /device:TPU:0, one launch (start us, length us, event | category | flops | bytes accessed | tf_op | source)
XLA Modules:
  0.0 121.3 jit_solution(15692697618177721500)
XLA Ops:
  0.0 1.0 convert_reduce_fusion
  1.0 0.7 multiply_add_fusion
  1.8 1.0 reshape.123
  2.8 0.4 fusion
  3.4 1.0 copy.86
  4.5 7.4 %all-to-all-start = ((bf16[16,3,4,16,128]{4,3,1,2,0:T(8,128)(2,1)}), bf16[16,3,4,16,128]{4,3,1,2,0:T(8,128)(2,1)S(1)}, u32[]{:S(2)}, u32[]{:S(2)}) async-start(bf16[16,3,4,16,128]{4,3,1,2,0:T(8,128)(2,1)} %copy.86), calls=%async_computation | async-start | bytes 1572864 | tf_op jit(solution)/shard_map/all_to_all | solution.py:258
  11.9 0.4 multiply_reduce_fusion.1
  12.4 18.2 %all-to-all-done = bf16[16,3,4,16,128]{4,3,1,2,0:T(8,128)(2,1)S(1)} async-done(((bf16[16,3,4,16,128]{4,3,1,2,0:T(8,128)(2,1)}), bf16[16,3,4,16,128]{4,3,1,2,0:T(8,128)(2,1)S(1)}, u32[]{:S(2)}, u32[]{:S(2)}) %all-to-all-start) | async-done | bytes 786464 | tf_op jit(solution)/shard_map/all_to_all | solution.py:258
  30.7 2.2 %copy-done = bf16[4096,512]{1,0:T(8,128)(2,1)S(1)} copy-done((bf16[4096,512]{1,0:T(8,128)(2,1)S(1)}, bf16[4096,512]{1,0:T(8,128)(2,1)}, u32[]{:S(2)}) %copy-start) | copy-done | bytes 4194328
  32.8 2.2 %copy-done.1 = bf16[4096,512]{1,0:T(8,128)(2,1)S(1)} copy-done((bf16[4096,512]{1,0:T(8,128)(2,1)S(1)}, bf16[4096,512]{1,0:T(8,128)(2,1)}, u32[]{:S(2)}) %copy-start.1) | copy-done | bytes 4194328
  35.0 19.6 %shard_map.73 = (bf16[4,768,128]{2,1,0:T(8,128)(2,1)S(1)}, f32[4,768,2]{2,1,0:T(8,128)S(1)}) custom-call(bf16[4,768,128]{2,1,0:T(8,128)(2,1)S(1)} %bitcast.67, bf16[4096,512]{1,0:T(8,128)(2,1)S(1)} %copy-done, bf16[4096,512]{1,0:T(8,128)(2,1)S(1)} %copy-done.1), custom_call_target="tpu_custom_call" | custom-call | tf_op jit(solution)/shard_map/pallas_call | solution.py:65
  54.7 1.3 %copy.88 = f32[4,16,3,16,2]{1,4,3,0,2:T(2,128)S(1)} copy(f32[4,16,3,16,2]{4,3,2,1,0:T(8,128)S(1)} %bitcast.68) | data formatting | bytes 49152 | tf_op jit(solution)/shard_map/reshape | solution.py:262
  55.9 0.7 copy.89
  56.6 5.5 %all-to-all-start.1 = ((f32[16,3,128]{2,1,0:T(4,128)}), f32[16,3,128]{2,1,0:T(4,128)S(1)}, u32[]{:S(2)}, u32[]{:S(2)}) async-start(f32[16,3,128]{2,1,0:T(4,128)} %copy.89), calls=%async_computation.1 | async-start | bytes 65536 | tf_op jit(solution)/shard_map/all_to_all | solution.py:265
  62.2 1.1 copy.107
  63.3 5.4 %all-to-all-done.1 = f32[16,3,128]{2,1,0:T(4,128)S(1)} async-done(((f32[16,3,128]{2,1,0:T(4,128)}), f32[16,3,128]{2,1,0:T(4,128)S(1)}, u32[]{:S(2)}, u32[]{:S(2)}) %all-to-all-start.1) | async-done | bytes 24608 | tf_op jit(solution)/shard_map/all_to_all | solution.py:265
  68.8 3.6 %all-to-all-start.2 = ((bf16[16,3,4,16,128]{4,3,2,1,0:T(8,128)(2,1)}), bf16[16,3,4,16,128]{4,3,2,1,0:T(8,128)(2,1)S(1)}, u32[]{:S(2)}, u32[]{:S(2)}) async-start(bf16[16,3,4,16,128]{4,3,2,1,0:T(8,128)(2,1)} %bitcast.66), calls=%async_computation.2 | async-start | bytes 1572864 | tf_op jit(solution)/shard_map/all_to_all | solution.py:264
  72.8 0.3 multiply_reduce_fusion
  73.9 17.1 %all-to-all-done.2 = bf16[16,3,4,16,128]{4,3,2,1,0:T(8,128)(2,1)S(1)} async-done(((bf16[16,3,4,16,128]{4,3,2,1,0:T(8,128)(2,1)}), bf16[16,3,4,16,128]{4,3,2,1,0:T(8,128)(2,1)S(1)}, u32[]{:S(2)}, u32[]{:S(2)}) %all-to-all-start.2) | async-done | bytes 786464 | tf_op jit(solution)/shard_map/all_to_all | solution.py:264
  91.0 0.3 reshape.130
  91.4 0.6 dot_general.12
  91.9 0.6 fusion.1
  92.9 27.7 %shard_map.74 = bf16[32,4096]{1,0:T(8,128)(2,1)S(1)} custom-call(bf16[32,2048]{1,0:T(8,128)(2,1)S(1)} %reshape.131.att_ref, bf16[2048,256]{1,0:T(8,128)(2,1)S(1)} %copy-done.2), custom_call_target="tpu_custom_call" | custom-call | tf_op jit(solution)/shard_map/pallas_call | solution.py:215
  120.6 0.7 copy.109
  (33 shorter events, 2.0 us)
Async XLA Ops:
  0.0 11.9 %copy-start.3 = (bf16[32,512]{1,0:T(8,128)(2,1)S(1)}, bf16[32,512]{1,0:T(8,128)(2,1)}, u32[]{:S(2)}) copy-start(bf16[32,512]{1,0:T(8,128)(2,1)} %param.8) | copy-start | bytes 98308
  4.5 26.1 %all-to-all-start = ((bf16[16,3,4,16,128]{4,3,1,2,0:T(8,128)(2,1)}), bf16[16,3,4,16,128]{4,3,1,2,0:T(8,128)(2,1)S(1)}, u32[]{:S(2)}, u32[]{:S(2)}) async-start(bf16[16,3,4,16,128]{4,3,1,2,0:T(8,128)(2,1)} %copy.86), calls=%async_computation | async-start | bytes 1572864 | tf_op jit(solution)/shard_map/all_to_all | solution.py:258
  30.7 2.2 %copy-start = (bf16[4096,512]{1,0:T(8,128)(2,1)S(1)}, bf16[4096,512]{1,0:T(8,128)(2,1)}, u32[]{:S(2)}) copy-start(bf16[4096,512]{1,0:T(8,128)(2,1)} %k_ref.1) | copy-start | bytes 12582916
  32.8 2.2 %copy-start.1 = (bf16[4096,512]{1,0:T(8,128)(2,1)S(1)}, bf16[4096,512]{1,0:T(8,128)(2,1)}, u32[]{:S(2)}) copy-start(bf16[4096,512]{1,0:T(8,128)(2,1)} %v_ref.1) | copy-start | bytes 12582916
  35.0 27.1 %copy-start.4 = (bf16[32,512]{1,0:T(8,128)(2,1)S(1)}, bf16[32,512]{1,0:T(8,128)(2,1)}, u32[]{:S(2)}) copy-start(bf16[32,512]{1,0:T(8,128)(2,1)} %param.9) | copy-start | bytes 98308
  56.6 12.1 %all-to-all-start.1 = ((f32[16,3,128]{2,1,0:T(4,128)}), f32[16,3,128]{2,1,0:T(4,128)S(1)}, u32[]{:S(2)}, u32[]{:S(2)}) async-start(f32[16,3,128]{2,1,0:T(4,128)} %copy.89), calls=%async_computation.1 | async-start | bytes 65536 | tf_op jit(solution)/shard_map/all_to_all | solution.py:265
  68.8 22.3 %all-to-all-start.2 = ((bf16[16,3,4,16,128]{4,3,2,1,0:T(8,128)(2,1)}), bf16[16,3,4,16,128]{4,3,2,1,0:T(8,128)(2,1)S(1)}, u32[]{:S(2)}, u32[]{:S(2)}) async-start(bf16[16,3,4,16,128]{4,3,2,1,0:T(8,128)(2,1)} %bitcast.66), calls=%async_computation.2 | async-start | bytes 1572864 | tf_op jit(solution)/shard_map/all_to_all | solution.py:264
  73.7 19.2 %copy-start.2 = (bf16[2048,256]{1,0:T(8,128)(2,1)S(1)}, bf16[2048,256]{1,0:T(8,128)(2,1)}, u32[]{:S(2)}) copy-start(bf16[2048,256]{1,0:T(8,128)(2,1)} %w_ref.1) | copy-start | bytes 3145732

commit v3 on v2

--- a/solution.py
+++ b/solution.py
@@ -47,38 +47,163 @@
     return acc / total, high * SCALE, total
 
 
-def page_kernel(block, chunk, q_ref, k_ref, v_ref, out_ref, stat_ref):
-    @pl.loop(0, q_ref.shape[1] // block)
+def asked_kernel(
+    n, group, chunk, q_ref, k_hbm, v_hbm, got, got_stat, asked, answer, stat, stat_out, k_buf, v_buf,
+    kv_sem, q_send, q_recv, o_send, o_recv, t_send, t_recv,
+):
+    me = lax.axis_index("seq")
+    unit = q_ref.shape[2]
+    blocks = n // group
+    mesh_id = pl.DeviceIdType.MESH
+
+    def page(g, src, buf, which):
+        return pltpu.make_async_copy(
+            src.at[:, g * HD : (g + 1) * HD], buf.at[g], kv_sem.at[which, g]
+        )
+
+    for g in range(KVH):
+        page(g, k_hbm, k_buf, 0).start()
+        page(g, v_hbm, v_buf, 1).start()
+
+    barrier = pltpu.get_barrier_semaphore()
+
+    @pl.loop(0, n - 1)
     def _(i):
-        rows = pl.ds(pl.multiple_of(i * block, block), block)
-        out, high, total = flash_rows(q_ref[0, rows, :], k_ref, v_ref, chunk)
-        out_ref[0, rows, :] = out.astype(out_ref.dtype)
-        stat_ref[0, rows, 0:1] = high
-        stat_ref[0, rows, 1:2] = total
-
-
-def page_attention(q, keys, values):
-    rows = q.shape[1]
+        pl.semaphore_signal(
+            barrier, inc=1, device_id={"seq": lax.rem(me + 1 + i, n)}, device_id_type=mesh_id
+        )
+
+    for g in range(KVH):
+        asked[g, pl.ds(me, 1)] = q_ref[g, pl.ds(me, 1)]
+    pl.semaphore_wait(barrier, n - 1)
+
+    def ask(g, d):
+        return pltpu.make_async_remote_copy(
+            src_ref=q_ref.at[g, d], dst_ref=asked.at[g, me],
+            send_sem=q_send.at[g, d], recv_sem=q_recv.at[g, me],
+            device_id={"seq": d}, device_id_type=mesh_id,
+        )
+
+    def asked_by(g, d):
+        return pltpu.make_async_remote_copy(
+            src_ref=q_ref.at[g, d], dst_ref=asked.at[g, d],
+            send_sem=q_send.at[g, d], recv_sem=q_recv.at[g, d],
+            device_id={"seq": d}, device_id_type=mesh_id,
+        )
+
+    def reply(g, d):
+        return pltpu.make_async_remote_copy(
+            src_ref=answer.at[g, d], dst_ref=got.at[g, me],
+            send_sem=o_send.at[g, d], recv_sem=o_recv.at[g, me],
+            device_id={"seq": d}, device_id_type=mesh_id,
+        )
+
+    def replied_by(g, d):
+        return pltpu.make_async_remote_copy(
+            src_ref=answer.at[g, d], dst_ref=got.at[g, d],
+            send_sem=o_send.at[g, d], recv_sem=o_recv.at[g, d],
+            device_id={"seq": d}, device_id_type=mesh_id,
+        )
+
+    def note(d, slot):
+        return pltpu.make_async_remote_copy(
+            src_ref=stat_out.at[d], dst_ref=got_stat.at[slot],
+            send_sem=t_send.at[d], recv_sem=t_recv.at[slot],
+            device_id={"seq": d}, device_id_type=mesh_id,
+        )
+
+    @pl.loop(0, KVH)
+    def _(g):
+        @pl.loop(0, n - 1)
+        def _(i):
+            ask(g, lax.rem(me + 1 + i, n)).start()
+
+    lane = lax.broadcasted_iota(jnp.int32, (group, unit, 128), 2)
+    row = lax.broadcasted_iota(jnp.int32, (group, unit, 128), 1)
+    diagonal = lane == row
+
+    def line(column):
+        spread = jnp.broadcast_to(column, (group * unit, 128)).reshape(group, unit, 128)
+        return jnp.sum(jnp.where(diagonal, spread, 0.0), axis=1)
+
+    for g in range(KVH):
+        page(g, k_hbm, k_buf, 0).wait()
+        page(g, v_hbm, v_buf, 1).wait()
+
+        @pl.loop(0, blocks)
+        def _(i):
+            first = pl.multiple_of(lax.rem(me // group + i, blocks) * group, group)
+
+            @pl.loop(0, group)
+            def _(j):
+                @pl.when(first + j != me)
+                def _():
+                    asked_by(g, first + j).wait_recv()
+
+            q = asked[g, pl.ds(first, group)].reshape(group * unit, HD)
+            out, high, total = flash_rows(q, k_buf.at[g], v_buf.at[g], chunk)
+            answer[g, pl.ds(first, group)] = out.astype(jnp.bfloat16).reshape(group, unit, HD)
+            stat[2 * g, pl.ds(first, group), :] = line(high)
+            stat[2 * g + 1, pl.ds(first, group), :] = line(total)
+
+            @pl.loop(0, group)
+            def _(j):
+                @pl.when(first + j != me)
+                def _():
+                    reply(g, first + j).start()
+
+    for d in range(n):
+        stat_out[d] = stat[:, d, :]
+
+    @pl.loop(0, n - 1)
+    def _(i):
+        note(lax.rem(me + 1 + i, n), me).start()
+
+    for g in range(KVH):
+        got[g, pl.ds(me, 1)] = answer[g, pl.ds(me, 1)]
+    got_stat[pl.ds(me, 1)] = stat_out[pl.ds(me, 1)]
+
+    @pl.loop(0, n - 1)
+    def _(i):
+        d = lax.rem(me + 1 + i, n)
+        for g in range(KVH):
+            ask(g, d).wait_send()
+            reply(g, d).wait_send()
+            replied_by(g, d).wait_recv()
+        note(d, d).wait_recv()
+        note(d, me).wait_send()
+
+
+def page_answers(q, keys, values):
+    n = lax.axis_size("seq")
+    unit = q.shape[2]
     page = keys.shape[0]
-    block = next(b for b in (256, 128, 64, 16) if rows % b == 0)
+    group = next(b for b in (16, 8, 4, 2, 1) if n % b == 0 and b * unit <= 384)
     chunk = next(c for c in (1024, 512, page) if page % c == 0)
+    vmem = pl.BlockSpec(memory_space=pltpu.VMEM)
+    hbm = pl.BlockSpec(memory_space=pl.ANY)
+    dma = pltpu.SemaphoreType.DMA
     return pl.pallas_call(
-        functools.partial(page_kernel, block, chunk),
-        grid=(KVH,),
-        in_specs=[
-            pl.BlockSpec((1, rows, HD), lambda g: (g, 0, 0)),
-            pl.BlockSpec((page, HD), lambda g: (0, g)),
-            pl.BlockSpec((page, HD), lambda g: (0, g)),
+        functools.partial(asked_kernel, n, group, chunk),
+        out_shape=[
+            jax.ShapeDtypeStruct((KVH, n, unit, HD), jnp.bfloat16),
+            jax.ShapeDtypeStruct((n, 2 * KVH, 128), jnp.float32),
         ],
-        out_specs=[
-            pl.BlockSpec((1, rows, HD), lambda g: (g, 0, 0)),
-            pl.BlockSpec((1, rows, 2), lambda g: (g, 0, 0)),
+        in_specs=[vmem, hbm, hbm],
+        out_specs=[vmem, vmem],
+        scratch_shapes=[
+            pltpu.VMEM((KVH, n, unit, HD), jnp.bfloat16),
+            pltpu.VMEM((KVH, n, unit, HD), jnp.bfloat16),
+            pltpu.VMEM((2 * KVH, n, 128), jnp.float32),
+            pltpu.VMEM((n, 2 * KVH, 128), jnp.float32),
+            pltpu.VMEM((KVH, page, HD), jnp.bfloat16),
+            pltpu.VMEM((KVH, page, HD), jnp.bfloat16),
+            dma((2, KVH)), dma((KVH, n)), dma((KVH, n)), dma((KVH, n)), dma((KVH, n)),
+            dma((n,)), dma((n,)),
         ],
-        out_shape=[
-            jax.ShapeDtypeStruct((KVH, rows, HD), jnp.bfloat16),
-            jax.ShapeDtypeStruct((KVH, rows, 2), jnp.float32),
-        ],
-        compiler_params=pltpu.CompilerParams(vmem_limit_bytes=40 * 1024 * 1024),
+        compiler_params=pltpu.CompilerParams(
+            collective_id=1, has_side_effects=True, vmem_limit_bytes=48 * 1024 * 1024
+        ),
     )(q, keys, values)
 
 
@@ -250,19 +375,12 @@
     asked = asked.reshape(tiles, KVH, unit, HD)
     outgoing = lax.dot_general(
         placing,
-        asked.reshape(tiles, -1),
-        (((0,), (0,)), ((), ())),
+        asked.transpose(1, 0, 2, 3).reshape(KVH, tiles, unit * HD),
+        (((0,), (1,)), ((), ())),
         preferred_element_type=jnp.float32,
     ).astype(jnp.bfloat16)
-    outgoing = outgoing.reshape(members, capacity, KVH, unit, HD)
-    incoming = lax.all_to_all(outgoing, "seq", split_axis=0, concat_axis=0, tiled=True)
-    incoming = incoming.transpose(2, 0, 1, 3, 4).reshape(KVH, slots * unit, HD)
-    out, stat = page_attention(incoming, keys, values)
-    out = out.reshape(KVH, members, capacity, unit, HD).transpose(1, 2, 0, 3, 4)
-    stat = stat.reshape(KVH, members, capacity, unit, 2).transpose(1, 2, 0, 3, 4)
-    stat = stat.reshape(members, capacity, KVH * unit * 2)
-    got = lax.all_to_all(out, "seq", split_axis=0, concat_axis=0, tiled=True)
-    got_stat = lax.all_to_all(stat, "seq", split_axis=0, concat_axis=0, tiled=True)
+    outgoing = outgoing.transpose(1, 0, 2).reshape(KVH, members, capacity * unit, HD)
+    got, got_stat = page_answers(outgoing, keys, values)
     a = asked.reshape(tiles, KVH, rows, PER, HD).astype(jnp.float32)
     nk = new_keys.reshape(tiles, rows, KVH, HD).transpose(0, 2, 1, 3).astype(jnp.float32)
     nv = new_values.reshape(tiles, rows, KVH, HD).transpose(0, 2, 1, 3).astype(jnp.float32)
@@ -278,11 +396,12 @@
     pick = slot_index[:, :, None] == jnp.arange(slots, dtype=jnp.int32)
     chosen = lax.dot_general(
         pick.reshape(tiles * width, slots).astype(jnp.bfloat16),
-        got.reshape(slots, KVH * unit * HD),
-        (((1,), (0,)), ((), ())),
+        got.reshape(KVH, slots, unit * HD),
+        (((1,), (1,)), ((), ())),
         preferred_element_type=jnp.float32,
     ).reshape(tiles, width, KVH, rows, PER, HD)
-    got_stat = got_stat.reshape(slots, KVH, rows, PER, 2)
+    got_stat = got_stat[:, :, : capacity * unit].reshape(members, KVH, 2, capacity, unit)
+    got_stat = got_stat.transpose(0, 3, 1, 4, 2)
     chosen_stat = jnp.sum(
         jnp.where(pick[..., None], got_stat.reshape(slots, -1)[None, None], 0.0), axis=2
     ).reshape(tiles, width, KVH, rows, PER, 2)

time: 122 us -> 86.2 us (0.71)
  waiting for transfers between devices: 40.8 us -> 0 us
  Pallas kernels: 47.3 us -> 73.8 us
  starting transfers between devices: 16.5 us -> 0 us
  local copies, waits for them, and re-layouts: 11.9 us -> 7.44 us
    all_to_all x3 -> x0, waiting for transfers between devices: 40.8 us -> none  [the longest x1 18.2 us: shards(): lax.all_to_all(outgoing, 'seq', split_axis=0, concat_axis=0, tiled=True)]
    pallas_call x1, Pallas kernels: 19.6 us -> 46.2 us  [page_answers(): pl.pallas_call(functools.partial(asked_kernel, n, group, chunk), out_shap...]
    all_to_all x3 -> x0, starting transfers between devices: 16.5 us -> none  [the longest x1 7.39 us: shards(): lax.all_to_all(outgoing, 'seq', split_axis=0, concat_axis=0, tiled=True)]
    reshape x5 -> x3, local copies, waits for them, and re-layouts: 4.45 us -> 0.84 us  [the longest x1 0.36 us: shards(): outgoing.transpose(1, 0, 2).reshape(KVH, members, capacity * unit, HD)]
    unnamed x12 -> x9, local copies, waits for them, and re-layouts: 5.27 us -> 2.9 us
  transfers between devices with their start and end apart: 3 -> 0, of which waited for: 3 -> 0; matrix products, arithmetic and copies ran while one was open for 3% -> 0% of each run, Pallas kernels for 0% -> 0%
where the time goes in v3:
time: 86.2 us; the launch traced here: 85.9 us
  Pallas kernels  73.8 us (86%)
  local copies, waits for them, and re-layouts  7.44 us (9%)
  other arithmetic  3.65 us (4%)
    pallas_call x1, Pallas kernels, page_answers(): pl.pallas_call(functools.partial(asked_kernel, n, group, chunk), out_shap...  46.2 us
    pallas_call x1, Pallas kernels, project(): pl.pallas_call(functools.partial(project_kernel, n), out_shape=jax.ShapeD...  27.7 us
    unnamed x9, local copies, waits for them, and re-layouts  2.9 us

profile of v3, /device:TPU:0, one launch (start us, length us, event | category | flops | bytes accessed | tf_op | source)
XLA Modules:
  0.0 85.9 jit_solution(14246923518210321007)
XLA Ops:
  0.0 1.0 %reshape.120 = bf16[8,4,4,4,128]{4,3,2,1,0:T(4,128)(2,1)S(1)} reshape(bf16[32,2048]{1,0:T(8,128)(2,1)} %param.7) | data formatting | bytes 262144 | tf_op jit(solution)/shard_map/reshape | solution.py:374
  1.0 0.1 bitcast_convert_fusion
  1.1 1.0 %convert_reduce_fusion = s32[8,3]{0,1:T(4,128)S(1)} fusion(s32[8,3]{0,1:T(4,128)} %param.12, pred[8,8]{1,0:T(8,128)(4,1)S(1)} %iota_compare_fusion.2), kind=kLoop, calls=%fused_computation.23 | loop fusion | flops 2280 | bytes 256 | tf_op jit(solution)/shard_map/reduce_sum | solution.py:369
  2.1 0.7 multiply_add_fusion
  2.8 0.4 fusion
  3.2 0.4 reshape.123.q_ref
  3.6 2.2 %copy-done = bf16[4096,512]{1,0:T(8,128)(2,1)S(1)} copy-done((bf16[4096,512]{1,0:T(8,128)(2,1)S(1)}, bf16[4096,512]{1,0:T(8,128)(2,1)}, u32[]{:S(2)}) %copy-start) | copy-done | bytes 4194328
  5.8 46.2 %shard_map.73 = (bf16[4,16,48,128]{3,2,1,0:T(8,128)(2,1)S(1)}, f32[16,8,128]{2,1,0:T(8,128)S(1)}) custom-call(bf16[4,16,48,128]{3,2,1,0:T(8,128)(2,1)S(1)} %reshape.123.q_ref, bf16[4096,512]{1,0:T(8,128)(2,1)S(1)} %copy-done, bf16[4096,512]{1,0:T(8,128)(2,1)} %v_hbm.1), custom_call_target="tpu_custom_call" | custom-call | tf_op jit(solution)/shard_map/pallas_call | solution.py:186
  52.0 0.3 reshape.126
  52.3 0.6 dot_general.12
  52.9 0.1 reshape.124
  53.1 1.1 %copy.75 = f32[16,3,4,16,2]{1,0,4,3,2:T(8,128)S(1)} copy(f32[16,3,4,16,2]{3,1,4,2,0:T(4,128)S(1)} %bitcast.72) | data formatting | bytes 49152 | tf_op jit(solution)/shard_map/transpose | solution.py:404
  54.1 0.5 broadcast_in_dim.30
  54.7 0.2 select_reduce_fusion
  55.0 0.1 copy.77
  55.1 0.2 fusion.17
  55.3 0.4 multiply_reduce_fusion.1
  55.8 0.2 fusion.6
  56.1 0.3 fusion.1
  56.5 0.2 fusion.7
  56.7 0.3 multiply_reduce_fusion
  57.2 0.2 fusion.5
  57.5 27.7 %shard_map.74 = bf16[32,4096]{1,0:T(8,128)(2,1)S(1)} custom-call(bf16[32,2048]{1,0:T(8,128)(2,1)S(1)} %reshape.127.att_ref, bf16[2048,256]{1,0:T(8,128)(2,1)S(1)} %copy-done.1), custom_call_target="tpu_custom_call" | custom-call | tf_op jit(solution)/shard_map/pallas_call | solution.py:340
  85.2 0.7 copy.92
  (23 shorter events, 0.6 us)
Async XLA Ops:
  3.6 2.2 %copy-start = (bf16[4096,512]{1,0:T(8,128)(2,1)S(1)}, bf16[4096,512]{1,0:T(8,128)(2,1)}, u32[]{:S(2)}) copy-start(bf16[4096,512]{1,0:T(8,128)(2,1)} %k_hbm.1) | copy-start | bytes 12582916
  52.0 3.3 %copy-start.2 = (bf16[32,512]{1,0:T(8,128)(2,1)S(1)}, bf16[32,512]{1,0:T(8,128)(2,1)}, u32[]{:S(2)}) copy-start(bf16[32,512]{1,0:T(8,128)(2,1)} %param.8) | copy-start | bytes 98308
  52.9 3.5 %copy-start.3 = (bf16[32,512]{1,0:T(8,128)(2,1)S(1)}, bf16[32,512]{1,0:T(8,128)(2,1)}, u32[]{:S(2)}) copy-start(bf16[32,512]{1,0:T(8,128)(2,1)} %param.9) | copy-start | bytes 98308
  54.6 2.9 %copy-start.1 = (bf16[2048,256]{1,0:T(8,128)(2,1)S(1)}, bf16[2048,256]{1,0:T(8,128)(2,1)}, u32[]{:S(2)}) copy-start(bf16[2048,256]{1,0:T(8,128)(2,1)} %w_ref.1) | copy-start | bytes 3145732

commit v4 on v3

--- a/solution.py
+++ b/solution.py
@@ -181,7 +181,7 @@
     group = next(b for b in (16, 8, 4, 2, 1) if n % b == 0 and b * unit <= 384)
     chunk = next(c for c in (1024, 512, page) if page % c == 0)
     vmem = pl.BlockSpec(memory_space=pltpu.VMEM)
-    hbm = pl.BlockSpec(memory_space=pl.ANY)
+    hbm = pl.BlockSpec(memory_space=pltpu.HBM)
     dma = pltpu.SemaphoreType.DMA
     return pl.pallas_call(
         functools.partial(asked_kernel, n, group, chunk),
@@ -254,7 +254,8 @@
             device_id={"seq": d}, device_id_type=pl.DeviceIdType.MESH,
         )
 
-    rights, lefts = chips // 2, (chips - 1) // 2
+    full = (chips - 1) // 2
+    hops = chips // 2
     started = []
 
     def project(c):
@@ -280,31 +281,40 @@
         copy.start()
         started.append(copy)
 
-    def step_right(s):
-        launch(move(chip_at(place - s) * 2 + core, right, r_send.at[s], r_recv.at[s]))
-
-    def step_left(s):
-        launch(move(chip_at(place + s) * 2 + core, left, l_send.at[s], l_recv.at[s]))
-
-    step_right(0)
-    if lefts:
-        step_left(0)
+    piece = held.shape[1] // 2
+
+    def hop(c, side, s, p):
+        part = held.at[
+            pl.ds(pl.multiple_of((c * 2 + core) * rows, rows), rows), p * piece : (p + 1) * piece
+        ]
+        send, recv, to = (r_send, r_recv, right) if side > 0 else (l_send, l_recv, left)
+        return pltpu.make_async_remote_copy(
+            src_ref=part, dst_ref=part, send_sem=send.at[s, p], recv_sem=recv.at[s, p],
+            device_id={"seq": to}, device_id_type=pl.DeviceIdType.MESH,
+        )
+
+    def pieces(side, s):
+        return (0, 1) if s < full else (0,) if side > 0 else (1,)
+
+    if hops:
+        for p in (0, 1):
+            for side in (1, -1):
+                if p in pieces(side, 0):
+                    launch(hop(chip, side, 0, p))
     launch(move(me, sibling, s_send.at[0], s_recv.at[0]))
     waiting = [(0, chip)]
     k = 1
-    for s in range(rights):
-        c = chip_at(place - 1 - s)
-        move(c * 2 + core, right, r_send.at[s], r_recv.at[s]).wait_recv()
-        if s + 1 < rights:
-            step_right(s + 1)
-        launch(move(c * 2 + core, sibling, s_send.at[k], s_recv.at[k]))
-        now = [(k, c)]
-        k += 1
-        if s < lefts:
-            c = chip_at(place + 1 + s)
-            move(c * 2 + core, left, l_send.at[s], l_recv.at[s]).wait_recv()
-            if s + 1 < lefts:
-                step_left(s + 1)
+    for s in range(hops):
+        for p in (0, 1):
+            for side in (1, -1):
+                c = chip_at(place - side * (1 + s))
+                if p in pieces(side, s):
+                    hop(c, side, s, p).wait_recv()
+                if s + 1 < hops and p in pieces(side, s + 1):
+                    launch(hop(c, side, s + 1, p))
+        now = []
+        for side in (1, -1) if s < full else (1,):
+            c = chip_at(place - side * (1 + s))
             launch(move(c * 2 + core, sibling, s_send.at[k], s_recv.at[k]))
             now.append((k, c))
             k += 1
@@ -346,7 +356,7 @@
             pltpu.VMEM((n * rows, features), jnp.bfloat16),
             pltpu.VMEM((n * rows, wide), jnp.bfloat16),
             pltpu.VMEM((n * rows, wide), jnp.bfloat16),
-            dma((chips,)), dma((chips,)), dma((chips,)), dma((chips,)),
+            dma((chips, 2)), dma((chips, 2)), dma((chips, 2)), dma((chips, 2)),
             dma((chips,)), dma((chips,)), dma((n,)), dma((n,)),
         ],
         compiler_params=pltpu.CompilerParams(

time: 86.2 us -> 85.8 us (level)
  no operation moved by 1% of the time
where the time goes in v4:
time: 85.8 us; the launch traced here: 85.6 us
  Pallas kernels  73.5 us (86%)
  local copies, waits for them, and re-layouts  7.44 us (9%)
  other arithmetic  3.65 us (4%)
    pallas_call x1, Pallas kernels, page_answers(): pl.pallas_call(functools.partial(asked_kernel, n, group, chunk), out_shap...  46.2 us
    pallas_call x1, Pallas kernels, project(): pl.pallas_call(functools.partial(project_kernel, n), out_shape=jax.ShapeD...  27.3 us
    unnamed x9, local copies, waits for them, and re-layouts  2.9 us

profile of v4, /device:TPU:0, one launch (start us, length us, event | category | flops | bytes accessed | tf_op | source)
XLA Modules:
  0.0 85.6 jit_solution(18352272907195600388)
XLA Ops:
  0.0 1.0 %reshape.120 = bf16[8,4,4,4,128]{4,3,2,1,0:T(4,128)(2,1)S(1)} reshape(bf16[32,2048]{1,0:T(8,128)(2,1)} %param.7) | data formatting | bytes 262144 | tf_op jit(solution)/shard_map/reshape | solution.py:384
  1.0 0.1 bitcast_convert_fusion
  1.1 1.0 %convert_reduce_fusion = s32[8,3]{0,1:T(4,128)S(1)} fusion(s32[8,3]{0,1:T(4,128)} %param.12, pred[8,8]{1,0:T(8,128)(4,1)S(1)} %iota_compare_fusion.2), kind=kLoop, calls=%fused_computation.23 | loop fusion | flops 2280 | bytes 256 | tf_op jit(solution)/shard_map/reduce_sum | solution.py:379
  2.1 0.7 multiply_add_fusion
  2.8 0.4 fusion
  3.2 0.4 reshape.123.q_ref
  3.6 2.2 %copy-done = bf16[4096,512]{1,0:T(8,128)(2,1)S(1)} copy-done((bf16[4096,512]{1,0:T(8,128)(2,1)S(1)}, bf16[4096,512]{1,0:T(8,128)(2,1)}, u32[]{:S(2)}) %copy-start) | copy-done | bytes 4194328
  5.8 46.2 %shard_map.73 = (bf16[4,16,48,128]{3,2,1,0:T(8,128)(2,1)S(1)}, f32[16,8,128]{2,1,0:T(8,128)S(1)}) custom-call(bf16[4,16,48,128]{3,2,1,0:T(8,128)(2,1)S(1)} %reshape.123.q_ref, bf16[4096,512]{1,0:T(8,128)(2,1)S(1)} %copy-done, bf16[4096,512]{1,0:T(8,128)(2,1)} %v_hbm.1), custom_call_target="tpu_custom_call" | custom-call | tf_op jit(solution)/shard_map/pallas_call | solution.py:186
  52.0 0.3 reshape.126
  52.3 0.6 dot_general.12
  52.9 0.1 reshape.124
  53.1 1.1 %copy.75 = f32[16,3,4,16,2]{1,0,4,3,2:T(8,128)S(1)} copy(f32[16,3,4,16,2]{3,1,4,2,0:T(4,128)S(1)} %bitcast.72) | data formatting | bytes 49152 | tf_op jit(solution)/shard_map/transpose | solution.py:414
  54.1 0.5 broadcast_in_dim.30
  54.7 0.2 select_reduce_fusion
  55.0 0.1 copy.77
  55.1 0.2 fusion.17
  55.3 0.4 multiply_reduce_fusion.1
  55.8 0.2 fusion.6
  56.1 0.3 fusion.1
  56.5 0.2 fusion.7
  56.7 0.3 multiply_reduce_fusion
  57.2 0.2 fusion.5
  57.5 27.3 %shard_map.74 = bf16[32,4096]{1,0:T(8,128)(2,1)S(1)} custom-call(bf16[32,2048]{1,0:T(8,128)(2,1)S(1)} %reshape.127.att_ref, bf16[2048,256]{1,0:T(8,128)(2,1)S(1)} %copy-done.1), custom_call_target="tpu_custom_call" | custom-call | tf_op jit(solution)/shard_map/pallas_call | solution.py:350
  84.9 0.7 copy.92
  (23 shorter events, 0.6 us)
Async XLA Ops:
  3.6 2.2 %copy-start = (bf16[4096,512]{1,0:T(8,128)(2,1)S(1)}, bf16[4096,512]{1,0:T(8,128)(2,1)}, u32[]{:S(2)}) copy-start(bf16[4096,512]{1,0:T(8,128)(2,1)} %k_hbm.1) | copy-start | bytes 12582916
  52.0 3.3 %copy-start.2 = (bf16[32,512]{1,0:T(8,128)(2,1)S(1)}, bf16[32,512]{1,0:T(8,128)(2,1)}, u32[]{:S(2)}) copy-start(bf16[32,512]{1,0:T(8,128)(2,1)} %param.8) | copy-start | bytes 98308
  52.9 3.5 %copy-start.3 = (bf16[32,512]{1,0:T(8,128)(2,1)S(1)}, bf16[32,512]{1,0:T(8,128)(2,1)}, u32[]{:S(2)}) copy-start(bf16[32,512]{1,0:T(8,128)(2,1)} %param.9) | copy-start | bytes 98308
  54.6 2.9 %copy-start.1 = (bf16[2048,256]{1,0:T(8,128)(2,1)S(1)}, bf16[2048,256]{1,0:T(8,128)(2,1)}, u32[]{:S(2)}) copy-start(bf16[2048,256]{1,0:T(8,128)(2,1)} %w_ref.1) | copy-start | bytes 3145732
